TPU v7x, 32 devices: a whole 2x2x4 slice. The times are simulated.
32 devices in a mesh: parts: 2 (over y), tensor: 4 (over z), dp: 4 (over x, core).
Axes of the slice: x: 2, y: 2, z: 4, core: 2. Of those that a mesh axis runs over, the one named last changes fastest.
Arguments:
- inputs_x: bfloat16 [8192, 4096], P(('parts', 'dp'), 'tensor'), parts along dimension 0, may hold values from -6 to 6
- hidden: bfloat16 [8192, 14336], P(('parts', 'dp'), 'tensor'), parts along dimension 0, may hold values from -6 to 6
- grad_gate: bfloat16 [8192, 14336], P(('parts', 'dp'), 'tensor'), parts along dimension 0, may hold values from -6 to 6
- grad_up: bfloat16 [8192, 14336], P(('parts', 'dp'), 'tensor'), parts along dimension 0, may hold values from -6 to 6
- grad_down: bfloat16 [8192, 4096], P(('parts', 'dp'), 'tensor'), parts along dimension 0, may hold values from -6 to 6
- proj_x: bfloat16 [4096, 128], P('tensor'), may hold values from -0.09375 to 0.09375
- proj_hidden: bfloat16 [14336, 64], P('tensor'), may hold values from -0.046875 to 0.046875
- proj_gate: bfloat16 [14336, 64], P('tensor'), may hold values from -0.046875 to 0.046875
- proj_up: bfloat16 [14336, 64], P('tensor'), may hold values from -0.046875 to 0.046875
- proj_down: bfloat16 [4096, 64], P('tensor'), may hold values from -0.09375 to 0.09375
- queries: bfloat16 [4096, 3, 4096], P('dp', None, 'tensor'), may hold values from -0.078125 to 0.078125
Outputs:
- scores: float32 [16, 4096], P(('parts', 'dp'), 'tensor'), parts along dimension 0
There are 2 independent parts, one for each index of `parts`. A program takes and returns all parts, laid end to end along the dimension named above; an argument that names none is the same for every part. Nothing has to cross between parts.
All inputs are finite; a program needn't handle non-finite values.
Results may differ from a plain program's by a relative error of at most 0.0003.
Values may be sent and summed in bfloat16 or wider, within the bound.
A program may use at most 128 MiB of HBM per device.

v0:
```python
import jax
import jax.numpy as jnp
from jax import lax
from jax.sharding import PartitionSpec as P

LEN = 512


def project(values, factors):
    return jnp.dot(values, factors, preferred_element_type=jnp.float32)


def shards(
    inputs_x,
    hidden,
    grad_gate,
    grad_up,
    grad_down,
    proj_x,
    proj_hidden,
    proj_gate,
    proj_up,
    proj_down,
    queries,
):
    local_terms = jnp.concatenate(
        [
            project(inputs_x, proj_x),
            project(hidden, proj_hidden),
            project(grad_gate, proj_gate),
            project(grad_up, proj_up),
            project(grad_down, proj_down),
        ],
        1,
    )
    tok_rows = local_terms.shape[0]
    project_width = proj_hidden.shape[1]
    devices = lax.axis_size("tensor")
    row_count = project_width // devices
    position = lax.axis_index("tensor")
    example_count = tok_rows // LEN
    factor = LEN ** (-0.5)
    summed = lax.psum(local_terms, "tensor")
    summed = summed.reshape(example_count, LEN, 2, 3, project_width)
    inputs_part = summed[:, :, 0]
    outputs_part = lax.dynamic_slice_in_dim(summed[:, :, 1], position * row_count, row_count, 3)
    gradients = jnp.einsum(
        "elmi,elmj->emij", outputs_part, inputs_part, precision=lax.Precision.HIGHEST
    )
    gradients = (gradients * factor).reshape(example_count, 3, row_count * project_width)
    score_terms = jnp.einsum(
        "emv,qmv->eq",
        gradients,
        lax.all_gather(queries, "dp", axis=0, tiled=True).astype(jnp.float32),
        precision=lax.Precision.HIGHEST,
    )
    return lax.psum_scatter(score_terms, "tensor", scatter_dimension=1, tiled=True)


def solution(mesh):
    placed = (
        P(("parts", "dp"), "tensor"),
        P(("parts", "dp"), "tensor"),
        P(("parts", "dp"), "tensor"),
        P(("parts", "dp"), "tensor"),
        P(("parts", "dp"), "tensor"),
        P("tensor", None),
        P("tensor", None),
        P("tensor", None),
        P("tensor", None),
        P("tensor", None),
        P("dp", None, "tensor"),
    )
    return jax.shard_map(
        shards, mesh=mesh, in_specs=placed, out_specs=P(("parts", "dp"), "tensor"), check_vma=False
    )
```

profile of v0, /device:TPU:0, one launch (start us, length us, event | category | flops | bytes accessed | tf_op | source)
XLA Modules:
  0.0 266.1 jit_solution(18170659084162232412)
XLA Ops:
  7.4 1.6 copy-done
  9.0 2.6 convolution_dynamic-update-slice_fusion
  11.5 6.3 %convolution_dynamic-update-slice_fusion.4 = f32[1024,384]{0,1:T(8,128)} fusion(f32[1024,384]{0,1:T(8,128)} %convolution_dynamic-update-slice_fusion, bf16[1024,3584]{1,0:T(8,128)(2,1)} %param.12, bf16[3584,64]{0,1:T(8,128)(2,1)S(1)} %copy-done.6), kind=kOutput, calls=%fused_computation.5 | convolution fusion | flops 469762048 | bytes 8060928 | tf_op jit(solution)/shard_map/dot_general | solution.py:10
  17.8 3.0 %convolution_dynamic-update-slice_fusion.3 = f32[1024,384]{0,1:T(8,128)} fusion(f32[1024,384]{0,1:T(8,128)} %convolution_dynamic-update-slice_fusion.4, bf16[1024,3584]{1,0:T(8,128)(2,1)S(1)} %copy-done.2, bf16[3584,64]{0,1:T(8,128)(2,1)S(1)} %copy-done.7), kind=kOutput, calls=%fused_computation.4 | convolution fusion | flops 469762048 | bytes 8060928 | tf_op jit(solution)/shard_map/dot_general | solution.py:10
  20.8 0.0 copy-done.3
  20.9 0.0 copy-done.8
  20.9 3.0 %convolution_dynamic-update-slice_fusion.2 = f32[1024,384]{0,1:T(8,128)} fusion(f32[1024,384]{0,1:T(8,128)} %convolution_dynamic-update-slice_fusion.3, bf16[1024,3584]{1,0:T(8,128)(2,1)S(1)} %copy-done.3, bf16[3584,64]{0,1:T(8,128)(2,1)S(1)} %copy-done.8), kind=kOutput, calls=%fused_computation.3 | convolution fusion | flops 469762048 | bytes 8060928 | tf_op jit(solution)/shard_map/dot_general | solution.py:10
  24.0 1.5 convolution_dynamic-update-slice_fusion.1
  25.4 2.6 reshape.7
  28.0 1.4 copy.16
  29.5 0.0 all-reduce.2.cloned.1.call-update
  29.5 0.0 all-gather.2.cloned.1.call-start
  29.6 0.5 all-gather.2.cloned.1.call-update
  30.1 0.0 reduce-scatter.4.cloned.1.call-start
  30.2 71.3 %all-reduce.2.cloned.1.call-done = f32[2,512,2,3,64]{1,4,3,0,2:T(8,128)} async-done(((f32[2,512,2,3,64]{1,4,3,0,2:T(8,128)}), f32[2,512,2,3,64]{1,4,3,0,2:T(8,128)}) %all-reduce.2.cloned.1.call-update) | async-done | bytes 1572880 | tf_op jit(solution)/shard_map/psum | solution.py:43
  101.5 1.3 slice.8
  102.8 0.3 copy-done.5
  103.1 0.7 convolution_multiply_fusion
  103.9 0.1 reshape.10
  104.0 85.0 %all-gather.2.cloned.1.call-done = bf16[4096,3,1024]{2,0,1:T(8,128)(2,1)} async-done(((bf16[1024,3,1024]{2,0,1:T(8,128)(2,1)}), bf16[4096,3,1024]{2,0,1:T(8,128)(2,1)}) %all-gather.2.cloned.1.call-update) | async-done | bytes 25165840 | tf_op jit(solution)/shard_map/all_gather | solution.py:54
  189.0 23.8 %convolution_bitcast_fusion = f32[4096,2]{1,0:T(8,128)} fusion(bf16[4096,3,1024]{2,0,1:T(8,128)(2,1)} %all-gather.2.cloned.1.call-done, f32[2,3,1024]{2,1,0:T(4,128)S(1)} %reshape.10), kind=kOutput, calls=%fused_computation | convolution fusion | flops 301989888 | bytes 25223168 | tf_op jit(solution)/shard_map/emv,qmv->eq/dot_general | solution.py:51
  212.8 0.0 reduce-scatter.4.cloned.1.call-update
  212.8 44.0 %reduce-scatter.4.cloned.1.call-done = f32[1024,2]{1,0:T(8,128)} async-done(((f32[4096,2]{1,0:T(8,128)}), f32[1024,2]{1,0:T(8,128)}) %reduce-scatter.4.cloned.1.call-update) | async-done | bytes 8208
  256.9 1.8 copy.20
  (17 shorter events, 0.0 us)
Async XLA Ops:
  7.4 1.6 copy-start
  7.4 4.2 %copy-start.6 = (bf16[3584,64]{0,1:T(8,128)(2,1)S(1)}, bf16[3584,64]{0,1:T(8,128)(2,1)}, u32[]{:S(2)}) copy-start(bf16[3584,64]{0,1:T(8,128)(2,1)} %param.17) | copy-start | bytes 1376260
  7.4 94.1 %all-reduce.2.cloned.1.call-start = ((), (), s32[]{:S(2)}) async-start(), calls=%async_computation.1 | async-start | bytes 3145728 | tf_op jit(solution)/shard_map/psum | solution.py:43
  11.5 6.3 %copy-start.2 = (bf16[1024,3584]{1,0:T(8,128)(2,1)S(1)}, bf16[1024,3584]{1,0:T(8,128)(2,1)}, u32[]{:S(2)}) copy-start(bf16[1024,3584]{1,0:T(8,128)(2,1)} %param.13) | copy-start | bytes 22020100
  11.5 6.3 %copy-start.7 = (bf16[3584,64]{0,1:T(8,128)(2,1)S(1)}, bf16[3584,64]{0,1:T(8,128)(2,1)}, u32[]{:S(2)}) copy-start(bf16[3584,64]{0,1:T(8,128)(2,1)} %param.18) | copy-start | bytes 1376260
  17.8 3.1 %copy-start.3 = (bf16[1024,3584]{1,0:T(8,128)(2,1)S(1)}, bf16[1024,3584]{1,0:T(8,128)(2,1)}, u32[]{:S(2)}) copy-start(bf16[1024,3584]{1,0:T(8,128)(2,1)} %param.14) | copy-start | bytes 22020100
  17.8 3.1 %copy-start.8 = (bf16[3584,64]{0,1:T(8,128)(2,1)S(1)}, bf16[3584,64]{0,1:T(8,128)(2,1)}, u32[]{:S(2)}) copy-start(bf16[3584,64]{0,1:T(8,128)(2,1)} %param.19) | copy-start | bytes 1376260
  20.9 3.0 %copy-start.4 = (bf16[1024,1024]{1,0:T(8,128)(2,1)S(1)}, bf16[1024,1024]{1,0:T(8,128)(2,1)}, u32[]{:S(2)}) copy-start(bf16[1024,1024]{1,0:T(8,128)(2,1)} %param.15) | copy-start | bytes 6291460
  20.9 3.0 %copy-start.9 = (bf16[1024,64]{0,1:T(8,128)(2,1)S(1)}, bf16[1024,64]{0,1:T(8,128)(2,1)}, u32[]{:S(2)}) copy-start(bf16[1024,64]{0,1:T(8,128)(2,1)} %param.20) | copy-start | bytes 393220
  29.5 159.5 %all-gather.2.cloned.1.call-start = ((), (), s32[]{:S(2)}) async-start(), calls=%async_computation.2 | async-start | bytes 31457280 | tf_op jit(solution)/shard_map/all_gather | solution.py:54
  30.1 226.8 %reduce-scatter.4.cloned.1.call-start = ((), (), s32[]{:S(2)}) async-start(), calls=%async_computation.3 | async-start | bytes 2621440
  101.5 1.6 copy-start.5
  189.0 69.7 %copy-start.1 = (bf16[1024,1024]{1,0:T(8,128)(2,1)S(1)}, bf16[1024,1024]{1,0:T(8,128)(2,1)}, u32[]{:S(2)}) copy-start(bf16[1024,1024]{1,0:T(8,128)(2,1)} %param.11) | copy-start | bytes 6291460
Sparse Core Ops, SparseCore 0:
  29.6 71.8 all-reduce.1
  212.9 43.8 reduce-scatter.3
Sparse Core Ops, SparseCore 1:
  31.6 157.4 all-gather.1
where the time goes:
time: 266 us
  waiting for transfers between devices  201 us (76%)
  matrix products  40.9 us (15%)
  between operations  14.9 us (6%)
  local copies, waits for them, and re-layouts  9.32 us (4%)
    all_gather x1, waiting for transfers between devices, shards(): lax.all_gather(queries, 'dp', axis=0, tiled=True).astype(jnp.float32)  85 us
    psum x1, waiting for transfers between devices, shards(): summed = lax.psum(local_terms, 'tensor')  71.3 us
    unnamed x4, waiting for transfers between devices  44.6 us
    dot_general x1, matrix products, shards(): jnp.einsum('emv,qmv->eq', gradients, lax.all_gather(queries, 'dp', axis=0...  23.8 us
    dot_general x5, matrix products, project(): return jnp.dot(values, factors, preferred_element_type=jnp.float32)  16.3 us
  transfers between devices with their start and end apart: 3, of which 3 were waited for; matrix products, arithmetic and copies ran while one was open for 1% of the time, Pallas kernels for 0%

commit v1 on v0

--- a/solution.py
+++ b/solution.py
@@ -33,28 +33,33 @@
         ],
         1,
     )
-    tok_rows = local_terms.shape[0]
-    project_width = proj_hidden.shape[1]
+    width = proj_hidden.shape[1]
     devices = lax.axis_size("tensor")
-    row_count = project_width // devices
-    position = lax.axis_index("tensor")
-    example_count = tok_rows // LEN
+    groups = lax.axis_size("dp")
+    examples = local_terms.shape[0] // LEN
     factor = LEN ** (-0.5)
-    summed = lax.psum(local_terms, "tensor")
-    summed = summed.reshape(example_count, LEN, 2, 3, project_width)
-    inputs_part = summed[:, :, 0]
-    outputs_part = lax.dynamic_slice_in_dim(summed[:, :, 1], position * row_count, row_count, 3)
+    summed = lax.psum_scatter(
+        local_terms.reshape(examples, devices, LEN // devices, 6 * width),
+        "tensor",
+        scatter_dimension=1,
+        tiled=True,
+    )
+    summed = summed.reshape(examples, LEN // devices, 2, 3, width)
     gradients = jnp.einsum(
-        "elmi,elmj->emij", outputs_part, inputs_part, precision=lax.Precision.HIGHEST
+        "elmi,elmj->emij", summed[:, :, 1], summed[:, :, 0], precision=lax.Precision.HIGHEST
     )
-    gradients = (gradients * factor).reshape(example_count, 3, row_count * project_width)
-    score_terms = jnp.einsum(
-        "emv,qmv->eq",
-        gradients,
-        lax.all_gather(queries, "dp", axis=0, tiled=True).astype(jnp.float32),
-        precision=lax.Precision.HIGHEST,
-    )
-    return lax.psum_scatter(score_terms, "tensor", scatter_dimension=1, tiled=True)
+    gradients = lax.psum_scatter(gradients * factor, "tensor", scatter_dimension=2, tiled=True)
+    gradients = gradients.reshape(examples, 3, width // devices * width)
+    gradients = lax.all_gather(gradients, "dp", axis=0, tiled=True)
+    high = lax.reduce_precision(gradients, 8, 7)
+    low = gradients - high
+    both = jnp.concatenate([high, low], 0).astype(jnp.bfloat16)
+    terms = jnp.einsum("emv,qmv->eq", both, queries, preferred_element_type=jnp.float32)
+    terms = terms[: examples * groups] + terms[examples * groups :]
+    scores = lax.psum(terms, "tensor")
+    scores = lax.all_to_all(scores, "dp", split_axis=0, concat_axis=1, tiled=True)
+    columns = scores.shape[1] // devices
+    return lax.dynamic_slice_in_dim(scores, lax.axis_index("tensor") * columns, columns, 1)
 
 
 def solution(mesh):

time: 266 us -> 132 us (0.50)
  waiting for transfers between devices: 201 us -> 60.6 us
  blocking collectives: 0 us -> 22.2 us
  matrix products: 40.9 us -> 23 us
  starting transfers between devices: 0.09 us -> 3.31 us
    all_gather x1 -> x0, waiting for transfers between devices: 85 us -> none  [shards(): lax.all_gather(queries, 'dp', axis=0, tiled=True).astype(jnp.float32)]
    psum x1 -> x0, waiting for transfers between devices: 71.3 us -> none  [shards(): summed = lax.psum(local_terms, 'tensor')]
    reduce_scatter x0 -> x2, waiting for transfers between devices: none -> 56.6 us  [the longest x1 38.1 us: shards(): lax.psum_scatter(local_terms.reshape(examples, devices, LEN // devices, 6...]
    unnamed x4 -> x2, waiting for transfers between devices: 44.6 us -> 0.03 us
    dot_general x2, matrix products: 24.5 us -> 6.65 us  [the longest x1 4.51 us: shards(): jnp.einsum('emv,qmv->eq', both, queries, preferred_element_type=jnp.float32)]
    psum x0 -> x1, blocking collectives: none -> 16.8 us  [shards(): scores = lax.psum(terms, 'tensor')]
    all_gather x0 -> x1, blocking collectives: none -> 5.43 us  [shards(): gradients = lax.all_gather(gradients, 'dp', axis=0, tiled=True)]
    all_to_all x0 -> x1, waiting for transfers between devices: none -> 3.91 us  [shards(): lax.all_to_all(scores, 'dp', split_axis=0, concat_axis=1, tiled=True)]
  transfers between devices with their start and end apart: 3 -> 3, of which waited for: 3 -> 3; matrix products, arithmetic and copies ran while one was open for 1% -> 0% of each run, Pallas kernels for 0% -> 0%
where the time goes in v1:
time: 132 us
  waiting for transfers between devices  60.6 us (46%)
  matrix products  23 us (17%)
  blocking collectives  22.2 us (17%)
  between operations  13.4 us (10%)
  local copies, waits for them, and re-layouts  9.05 us (7%)
  starting transfers between devices  3.31 us (3%)
    reduce_scatter x1, waiting for transfers between devices, shards(): lax.psum_scatter(local_terms.reshape(examples, devices, LEN // devices, 6...  38.1 us
    reduce_scatter x1, waiting for transfers between devices, shards(): lax.psum_scatter(gradients * factor, 'tensor', scatter_dimension=2, tiled...  18.5 us
    psum x1, blocking collectives, shards(): scores = lax.psum(terms, 'tensor')  16.8 us
    dot_general x5, matrix products, project(): return jnp.dot(values, factors, preferred_element_type=jnp.float32)  16.3 us
    reshape x2, local copies, waits for them, and re-layouts, shards(): local_terms.reshape(examples, devices, LEN // devices, 6 * width)  5.72 us
    all_gather x1, blocking collectives, shards(): gradients = lax.all_gather(gradients, 'dp', axis=0, tiled=True)  5.43 us
    dot_general x1, matrix products, shards(): jnp.einsum('emv,qmv->eq', both, queries, preferred_element_type=jnp.float32)  4.51 us
    all_to_all x1, waiting for transfers between devices, shards(): lax.all_to_all(scores, 'dp', split_axis=0, concat_axis=1, tiled=True)  3.91 us
  transfers between devices with their start and end apart: 3, of which 3 were waited for; matrix products, arithmetic and copies ran while one was open for 0% of the time, Pallas kernels for 0%

profile of v1, /device:TPU:0, one launch (start us, length us, event | category | flops | bytes accessed | tf_op | source)
XLA Modules:
  0.0 131.6 jit_solution(13266782308560299469)
XLA Ops:
  6.5 1.6 %copy-done = bf16[1024,1024]{1,0:T(8,128)(2,1)S(1)} copy-done((bf16[1024,1024]{1,0:T(8,128)(2,1)S(1)}, bf16[1024,1024]{1,0:T(8,128)(2,1)}, u32[]{:S(2)}) %copy-start) | copy-done | bytes 2097176
  8.1 2.6 %convolution_dynamic-update-slice_fusion = f32[1024,384]{0,1:T(8,128)} fusion(bf16[1024,1024]{1,0:T(8,128)(2,1)S(1)} %copy-done, bf16[1024,128]{1,0:T(8,128)(2,1)} %param.16), kind=kOutput, calls=%fused_computation | convolution fusion | flops 268435456 | bytes 2883584 | tf_op jit(solution)/shard_map/dot_general | solution.py:10
  10.7 6.3 %convolution_dynamic-update-slice_fusion.4 = f32[1024,384]{0,1:T(8,128)} fusion(f32[1024,384]{0,1:T(8,128)} %convolution_dynamic-update-slice_fusion, bf16[1024,3584]{1,0:T(8,128)(2,1)} %param.12, bf16[3584,64]{0,1:T(8,128)(2,1)S(1)} %copy-done.4), kind=kOutput, calls=%fused_computation.4 | convolution fusion | flops 469762048 | bytes 8060928 | tf_op jit(solution)/shard_map/dot_general | solution.py:10
  17.0 3.0 %convolution_dynamic-update-slice_fusion.3 = f32[1024,384]{0,1:T(8,128)} fusion(f32[1024,384]{0,1:T(8,128)} %convolution_dynamic-update-slice_fusion.4, bf16[1024,3584]{1,0:T(8,128)(2,1)S(1)} %copy-done.1, bf16[3584,64]{0,1:T(8,128)(2,1)S(1)} %copy-done.5), kind=kOutput, calls=%fused_computation.3 | convolution fusion | flops 469762048 | bytes 8060928 | tf_op jit(solution)/shard_map/dot_general | solution.py:10
  20.0 0.1 copy-done.2
  20.0 0.1 copy-done.6
  20.2 3.0 %convolution_dynamic-update-slice_fusion.2 = f32[1024,384]{0,1:T(8,128)} fusion(f32[1024,384]{0,1:T(8,128)} %convolution_dynamic-update-slice_fusion.3, bf16[1024,3584]{1,0:T(8,128)(2,1)S(1)} %copy-done.2, bf16[3584,64]{0,1:T(8,128)(2,1)S(1)} %copy-done.6), kind=kOutput, calls=%fused_computation.2 | convolution fusion | flops 469762048 | bytes 8060928 | tf_op jit(solution)/shard_map/dot_general | solution.py:10
  23.2 1.5 %convolution_dynamic-update-slice_fusion.1 = f32[1024,384]{0,1:T(8,128)} fusion(f32[1024,384]{0,1:T(8,128)} %convolution_dynamic-update-slice_fusion.2, bf16[1024,1024]{1,0:T(8,128)(2,1)S(1)} %copy-done.3, bf16[1024,64]{0,1:T(8,128)(2,1)S(1)} %copy-done.7), kind=kOutput, calls=%fused_computation.1 | convolution fusion | flops 134217728 | bytes 2490368 | tf_op jit(solution)/shard_map/dot_general | solution.py:10
  24.7 2.9 %reshape.12 = f32[2,4,128,384]{2,1,0,3:T(4,128)} reshape(f32[1024,384]{0,1:T(8,128)} %convolution_dynamic-update-slice_fusion.1) | data formatting | bytes 3145728 | tf_op jit(solution)/shard_map/reshape | solution.py:42
  27.6 2.9 %copy.19 = f32[2,4,128,384]{2,3,0,1:T(8,128)} copy(f32[2,4,128,384]{2,1,0,3:T(4,128)} %reshape.12) | data formatting | bytes 3145728 | tf_op jit(solution)/shard_map/reshape | solution.py:42
  30.4 0.0 reduce-scatter.3.cloned.1.call-update
  30.4 0.0 reduce-scatter.5.cloned.1.call-start
  30.5 38.1 %reduce-scatter.3.cloned.1.call-done = f32[2,1,128,384]{2,3,0,1:T(8,128)} async-done(((f32[2,4,128,384]{2,3,0,1:T(8,128)}), f32[2,1,128,384]{2,3,0,1:T(8,128)}) %reduce-scatter.3.cloned.1.call-update) | async-done | bytes 393232 | tf_op jit(solution)/shard_map/reduce_scatter | solution.py:41
  68.6 2.1 %convolution_multiply_fusion = f32[2,3,64,64]{3,2,1,0:T(8,128)} fusion(f32[2,128,2,3,64]{1,4,3,2,0:T(8,128)} %bitcast.31), kind=kOutput, calls=%fused_computation.5 | convolution fusion | flops 37773312 | bytes 491520 | tf_op jit(solution)/shard_map/elmi,elmj->emij/dot_general | solution.py:48
  70.7 0.0 reduce-scatter.5.cloned.1.call-update
  70.8 18.5 %reduce-scatter.5.cloned.1.call-done = f32[2,3,16,64]{3,2,1,0:T(8,128)} async-done(((f32[2,3,64,64]{3,2,1,0:T(8,128)}), f32[2,3,16,64]{3,2,1,0:T(8,128)}) %reduce-scatter.5.cloned.1.call-update) | async-done | bytes 24592 | tf_op jit(solution)/shard_map/reduce_scatter | solution.py:51
  89.3 0.9 reshape.16
  90.2 5.4 %all_gather.3 = f32[8,3,1024]{2,1,0:T(4,128)S(1)} all-gather(f32[2,3,1024]{2,1,0:T(4,128)S(1)} %reshape.16), channel_id=1, replica_groups=mesh['parts'=2,'tensor'=4,'dp'=4] {'dp'}, dimensions={0}, use_global_device_ids=true | all-gather | bytes 122880 | tf_op jit(solution)/shard_map/all_gather | solution.py:53
  95.6 0.1 reduce-precision_convert_fusion
  95.7 4.5 %convolution_bitcast_fusion = f32[16,1024]{1,0:T(8,128)S(1)} fusion(bf16[1024,3,1024]{2,0,1:T(8,128)(2,1)} %param.21, bf16[8,3,1024]{2,0,1:T(8,128)(2,1)S(1)} %get-tuple-element.6, bf16[8,3,1024]{2,0,1:T(8,128)(2,1)S(1)} %get-tuple-element.5), kind=kOutput, calls=%fused_computation.6 | convolution fusion | flops 100859904 | bytes 6455296 | tf_op jit(solution)/shard_map/emv,qmv->eq/dot_general | solution.py:57
  100.2 16.8 %psum.7 = f32[4,2,1024]{2,1,0:T(2,128)} all-reduce(f32[4,2,1024]{2,1,0:T(2,128)S(1)} %all_to_all.14), channel_id=1, replica_groups=mesh['parts'=2,'tensor'=4,'dp'=4] {'tensor'}, use_global_device_ids=true, to_apply=%region_2.0 | all-reduce | flops 8192 | bytes 65536 | tf_op jit(solution)/shard_map/psum | solution.py:59
  117.0 3.3 %all-to-all-start = ((f32[4,2,1024]{2,1,0:T(2,128)}), f32[4,2,1024]{2,1,0:T(2,128)S(1)}, u32[]{:S(2)}, u32[]{:S(2)}) async-start(f32[4,2,1024]{2,1,0:T(2,128)} %psum.7), calls=%async_computation.2 | async-start | bytes 65536 | tf_op jit(solution)/shard_map/all_to_all | solution.py:60
  120.3 3.9 %all-to-all-done = f32[4,2,1024]{2,1,0:T(2,128)S(1)} async-done(((f32[4,2,1024]{2,1,0:T(2,128)}), f32[4,2,1024]{2,1,0:T(2,128)S(1)}, u32[]{:S(2)}, u32[]{:S(2)}) %all-to-all-start) | async-done | bytes 32800 | tf_op jit(solution)/shard_map/all_to_all | solution.py:60
  124.2 0.6 constant_dynamic-slice_fusion
  (16 shorter events, 0.1 us)
Async XLA Ops:
  6.5 1.6 %copy-start = (bf16[1024,1024]{1,0:T(8,128)(2,1)S(1)}, bf16[1024,1024]{1,0:T(8,128)(2,1)}, u32[]{:S(2)}) copy-start(bf16[1024,1024]{1,0:T(8,128)(2,1)} %param.11) | copy-start | bytes 6291460
  6.5 4.2 %copy-start.4 = (bf16[3584,64]{0,1:T(8,128)(2,1)S(1)}, bf16[3584,64]{0,1:T(8,128)(2,1)}, u32[]{:S(2)}) copy-start(bf16[3584,64]{0,1:T(8,128)(2,1)} %param.17) | copy-start | bytes 1376260
  6.5 62.1 %reduce-scatter.3.cloned.1.call-start = ((), (), s32[]{:S(2)}) async-start(), calls=%async_computation.3 | async-start | bytes 1966080 | tf_op jit(solution)/shard_map/reduce_scatter | solution.py:41
  10.7 6.3 %copy-start.1 = (bf16[1024,3584]{1,0:T(8,128)(2,1)S(1)}, bf16[1024,3584]{1,0:T(8,128)(2,1)}, u32[]{:S(2)}) copy-start(bf16[1024,3584]{1,0:T(8,128)(2,1)} %param.13) | copy-start | bytes 22020100
  10.7 6.3 %copy-start.5 = (bf16[3584,64]{0,1:T(8,128)(2,1)S(1)}, bf16[3584,64]{0,1:T(8,128)(2,1)}, u32[]{:S(2)}) copy-start(bf16[3584,64]{0,1:T(8,128)(2,1)} %param.18) | copy-start | bytes 1376260
  17.0 3.1 %copy-start.2 = (bf16[1024,3584]{1,0:T(8,128)(2,1)S(1)}, bf16[1024,3584]{1,0:T(8,128)(2,1)}, u32[]{:S(2)}) copy-start(bf16[1024,3584]{1,0:T(8,128)(2,1)} %param.14) | copy-start | bytes 22020100
  17.0 3.2 %copy-start.6 = (bf16[3584,64]{0,1:T(8,128)(2,1)S(1)}, bf16[3584,64]{0,1:T(8,128)(2,1)}, u32[]{:S(2)}) copy-start(bf16[3584,64]{0,1:T(8,128)(2,1)} %param.19) | copy-start | bytes 1376260
  20.2 3.0 %copy-start.3 = (bf16[1024,1024]{1,0:T(8,128)(2,1)S(1)}, bf16[1024,1024]{1,0:T(8,128)(2,1)}, u32[]{:S(2)}) copy-start(bf16[1024,1024]{1,0:T(8,128)(2,1)} %param.15) | copy-start | bytes 6291460
  20.2 3.0 %copy-start.7 = (bf16[1024,64]{0,1:T(8,128)(2,1)S(1)}, bf16[1024,64]{0,1:T(8,128)(2,1)}, u32[]{:S(2)}) copy-start(bf16[1024,64]{0,1:T(8,128)(2,1)} %param.20) | copy-start | bytes 393220
  30.4 58.8 %reduce-scatter.5.cloned.1.call-start = ((), (), s32[]{:S(2)}) async-start(), calls=%async_computation.4 | async-start | bytes 245760 | tf_op jit(solution)/shard_map/reduce_scatter | solution.py:51
  117.0 7.2 %all-to-all-start = ((f32[4,2,1024]{2,1,0:T(2,128)}), f32[4,2,1024]{2,1,0:T(2,128)S(1)}, u32[]{:S(2)}, u32[]{:S(2)}) async-start(f32[4,2,1024]{2,1,0:T(2,128)} %psum.7), calls=%async_computation.2 | async-start | bytes 65536 | tf_op jit(solution)/shard_map/all_to_all | solution.py:60
Sparse Core Ops, SparseCore 0:
  30.6 37.9 reduce-scatter.2
  70.9 18.3 reduce-scatter.4

commit v2 on v0

v2 whole, which is shorter than its diff:
```python
import functools

import jax
import jax.numpy as jnp
from jax import lax
from jax.experimental import pallas as pl
from jax.experimental.pallas import tpu as pltpu
from jax.sharding import PartitionSpec as P

LEN = 512
MESH = pl.DeviceIdType.MESH
AHEAD = 2


def gradient_kernel(n, groups, examples, width, *refs):
    values, factors, out = refs[:5], refs[5:10], refs[10]
    held, weights = refs[11:16], refs[16:21]
    (terms, arrived, pieces, rows_in, shared, load_sem, weight_sem,
     send_sem, recv_sem, send2, recv2, send3, recv3) = refs[21:]
    me, lane = lax.axis_index("tensor"), lax.axis_index("dp")
    tokens = terms.shape[1]
    rows = width // n

    def load(step, k):
        owner = lax.rem(me + 1 + step, n)
        start = pl.multiple_of(owner * tokens, tokens)
        return pltpu.make_async_copy(
            values[k].at[pl.ds(start, tokens)], held[k].at[step], load_sem.at[step, k]
        )

    def weight(k):
        return pltpu.make_async_copy(factors[k], weights[k], weight_sem.at[k])

    for k in range(5):
        weight(k).start()
        load(0, k).start()
    for step in range(1, min(AHEAD, n)):
        for k in range(5):
            load(step, k).start()

    barrier = pltpu.get_barrier_semaphore()
    for hop in range(1, n):
        pl.semaphore_signal(barrier, inc=1, device_id={"tensor": lax.rem(me + hop, n)}, device_id_type=MESH)
    for hop in range(1, groups):
        pl.semaphore_signal(barrier, inc=1, device_id={"dp": lax.rem(lane + hop, groups)}, device_id_type=MESH)
    pl.semaphore_wait(barrier, n + groups - 2)
    for k in range(5):
        weight(k).wait()

    def send(step):
        return pltpu.make_async_remote_copy(
            src_ref=terms.at[step],
            dst_ref=arrived.at[step],
            send_sem=send_sem.at[step],
            recv_sem=recv_sem.at[step],
            device_id={"tensor": lax.rem(me + 1 + step, n)},
            device_id_type=MESH,
        )

    def project(step, carry):
        @pl.when(step + AHEAD < n)
        def _():
            for k in range(5):
                load(step + AHEAD, k).start()

        column = 0
        for k in range(5):
            load(step, k).wait()
            share = weights[k].shape[1]
            terms[step, :, column : column + share] = jnp.dot(
                held[k][step], weights[k][...], preferred_element_type=jnp.float32
            )
            column += share

        @pl.when(step < n - 1)
        def _():
            send(step).start()

        return carry

    lax.fori_loop(0, n, project, 0)

    total = terms[n - 1]
    for step in range(n - 1):
        send(step).wait_recv()
        total = total + arrived[step]
    product = lax.dot_general(
        total[:, 3 * width :],
        total[:, : 3 * width],
        (((0,), (0,)), ((), ())),
        precision=lax.Precision.HIGHEST,
        preferred_element_type=jnp.float32,
    ) * (LEN ** -0.5)
    for peer in range(n):
        for m in range(3):
            first = m * width + peer * rows
            pieces[peer, m] = product[first : first + rows, m * width : (m + 1) * width]

    def send_rows(hop):
        peer = lax.rem(me + hop, n)
        return pltpu.make_async_remote_copy(
            src_ref=pieces.at[peer],
            dst_ref=rows_in.at[me],
            send_sem=send2.at[hop - 1],
            recv_sem=recv2.at[hop - 1],
            device_id={"tensor": peer},
            device_id_type=MESH,
        )

    for hop in range(1, n):
        send_rows(hop).start()
    rows_in[me] = pieces[me]
    for hop in range(1, n):
        send_rows(hop).wait_recv()
    each = n // examples
    for e in range(examples):
        done = rows_in[e * each]
        for source in range(e * each + 1, (e + 1) * each):
            done = done + rows_in[source]
        shared[lane, e] = done

    def share(hop):
        return pltpu.make_async_remote_copy(
            src_ref=shared.at[lane],
            dst_ref=shared.at[lane],
            send_sem=send3.at[hop - 1],
            recv_sem=recv3.at[hop - 1],
            device_id={"dp": lax.rem(lane + hop, groups)},
            device_id_type=MESH,
        )

    for hop in range(1, groups):
        share(hop).start()
    for hop in range(1, groups):
        share(hop).wait_recv()
    out[...] = shared[...]
    for step in range(n - 1):
        send(step).wait_send()
    for hop in range(1, n):
        send_rows(hop).wait_send()
    for hop in range(1, groups):
        share(hop).wait_send()


def score_kernel(n, groups, examples, terms, out, blocks, arrived, send_sem, recv_sem):
    me, lane = lax.axis_index("tensor"), lax.axis_index("dp")
    split = n // groups
    columns = out.shape[1]
    source = me // split
    own = lane == source

    barrier = pltpu.get_barrier_semaphore()
    for t in range(n):
        @pl.when(jnp.logical_not(own & (me == t)))
        def _(t=t):
            pl.semaphore_signal(barrier, inc=1, device_id={"dp": source, "tensor": t}, device_id_type=MESH)

    for b in range(groups):
        for s in range(split):
            blocks[b * split + s] = (
                terms[b * examples : (b + 1) * examples, s * columns : (s + 1) * columns]
                + terms[
                    (groups + b) * examples : (groups + b + 1) * examples,
                    s * columns : (s + 1) * columns,
                ]
            )

    @pl.when(own)
    def _():
        pl.semaphore_wait(barrier, n - 1)

    @pl.when(jnp.logical_not(own))
    def _():
        pl.semaphore_wait(barrier, n)

    def send(b, s):
        return pltpu.make_async_remote_copy(
            src_ref=blocks.at[b * split + s],
            dst_ref=arrived.at[me],
            send_sem=send_sem.at[b * split + s],
            recv_sem=recv_sem.at[me],
            device_id={"dp": b, "tensor": lane * split + s},
            device_id_type=MESH,
        )

    def to_me(b, s):
        return (lane == b) & (me == lane * split + s)

    for b in range(groups):
        for s in range(split):
            @pl.when(jnp.logical_not(to_me(b, s)))
            def _(b=b, s=s):
                send(b, s).start()

            @pl.when(to_me(b, s))
            def _(b=b, s=s):
                arrived[me] = blocks[b * split + s]

    def wait_from(t):
        pltpu.make_async_remote_copy(
            src_ref=blocks.at[0],
            dst_ref=arrived.at[t],
            send_sem=send_sem.at[0],
            recv_sem=recv_sem.at[t],
            device_id={"dp": source, "tensor": t},
            device_id_type=MESH,
        ).wait_recv()

    for t in range(n):
        @pl.when(jnp.logical_not(own & (me == t)))
        def _(t=t):
            wait_from(t)

    total = arrived[0]
    for t in range(1, n):
        total = total + arrived[t]
    out[...] = total
    for b in range(groups):
        for s in range(split):
            @pl.when(jnp.logical_not(to_me(b, s)))
            def _(b=b, s=s):
                send(b, s).wait_send()


def shards(n, groups, *arrays):
    values, factors, queries = arrays[:5], arrays[5:10], arrays[10]
    width = factors[1].shape[1]
    local = values[0].shape[0]
    examples, tokens, rows = local // LEN, local // n, width // n
    f32, bf16 = jnp.float32, jnp.bfloat16
    dma = pltpu.SemaphoreType.DMA
    gradients = pl.pallas_call(
        functools.partial(gradient_kernel, n, groups, examples, width),
        out_shape=jax.ShapeDtypeStruct((groups, examples, 3, rows, width), f32),
        in_specs=[pl.BlockSpec(memory_space=pl.ANY)] * 10,
        out_specs=pl.BlockSpec(memory_space=pltpu.VMEM),
        scratch_shapes=[pltpu.VMEM((n, tokens, v.shape[1]), bf16) for v in values]
        + [pltpu.VMEM(w.shape, bf16) for w in factors]
        + [
            pltpu.VMEM((n, tokens, 6 * width), f32),
            pltpu.VMEM((n - 1, tokens, 6 * width), f32),
            pltpu.VMEM((n, 3, rows, width), f32),
            pltpu.VMEM((n, 3, rows, width), f32),
            pltpu.VMEM((groups, examples, 3, rows, width), f32),
            dma((n, 5)),
            dma((5,)),
            dma((n - 1,)),
            dma((n - 1,)),
            dma((n - 1,)),
            dma((n - 1,)),
            dma((groups - 1,)),
            dma((groups - 1,)),
        ],
        compiler_params=pltpu.CompilerParams(
            collective_id=0, has_side_effects=True, vmem_limit_bytes=56 * 2**20
        ),
    )(values[0], values[1], values[2], values[3], values[4], *factors)
    gradients = gradients.reshape(groups * examples, 3, rows * width)
    high = lax.reduce_precision(gradients, 8, 7)
    low = gradients - high
    both = jnp.concatenate([high, low], 0).astype(bf16)
    terms = jnp.einsum("emv,qmv->eq", both, queries, preferred_element_type=f32)
    columns = terms.shape[1] * groups // n
    return pl.pallas_call(
        functools.partial(score_kernel, n, groups, examples),
        out_shape=jax.ShapeDtypeStruct((examples, columns), f32),
        in_specs=[pl.BlockSpec(memory_space=pltpu.VMEM)],
        out_specs=pl.BlockSpec(memory_space=pltpu.VMEM),
        scratch_shapes=[
            pltpu.VMEM((n, examples, columns), f32),
            pltpu.VMEM((n, examples, columns), f32),
            dma((n,)),
            dma((n,)),
        ],
        compiler_params=pltpu.CompilerParams(collective_id=1, has_side_effects=True),
    )(terms)


def solution(mesh):
    placed = (
        P(("parts", "dp"), "tensor"),
        P(("parts", "dp"), "tensor"),
        P(("parts", "dp"), "tensor"),
        P(("parts", "dp"), "tensor"),
        P(("parts", "dp"), "tensor"),
        P("tensor", None),
        P("tensor", None),
        P("tensor", None),
        P("tensor", None),
        P("tensor", None),
        P("dp", None, "tensor"),
    )
    return jax.shard_map(
        functools.partial(shards, mesh.shape["tensor"], mesh.shape["dp"]),
        mesh=mesh,
        in_specs=placed,
        out_specs=P(("parts", "dp"), "tensor"),
        check_vma=False,
    )
```

time: 266 us -> 79.6 us (0.30)
  waiting for transfers between devices: 201 us -> 0 us
  Pallas kernels: 0 us -> 63.1 us
  matrix products: 40.9 us -> 5.14 us
  between operations: 14.9 us -> 0.03 us
    all_gather x1 -> x0, waiting for transfers between devices: 85 us -> none  [shards(): lax.all_gather(queries, 'dp', axis=0, tiled=True).astype(jnp.float32)]
    psum x1 -> x0, waiting for transfers between devices: 71.3 us -> none  [shards(): summed = lax.psum(local_terms, 'tensor')]
    pallas_call x0 -> x2, Pallas kernels: none -> 63.1 us  [the longest x1 56.1 us: shards(): pl.pallas_call(functools.partial(gradient_kernel, n, groups, examples, wi...]
    unnamed x4 -> x0, waiting for transfers between devices: 44.6 us -> none
    dot_general x7 -> x1, matrix products: 40.9 us -> 5.14 us  [shards(): terms = jnp.einsum('emv,qmv->eq', both, queries, preferred_element_type=f32)]
    unnamed x21 -> x5, local copies, waits for them, and re-layouts: 3.84 us -> 9.86 us
    reshape x3 -> x1, local copies, waits for them, and re-layouts: 4.17 us -> 1.05 us  [shards(): gradients = gradients.reshape(groups * examples, 3, rows * width)]
  transfers between devices with their start and end apart: 3 -> 0, of which waited for: 3 -> 0; matrix products, arithmetic and copies ran while one was open for 1% -> 0% of each run, Pallas kernels for 0% -> 0%
where the time goes in v2:
time: 79.6 us; the launch traced here: 79.2 us
  Pallas kernels  63.1 us (79%)
  local copies, waits for them, and re-layouts  10.9 us (14%)
  matrix products  5.14 us (6%)
    pallas_call x1, Pallas kernels, shards(): pl.pallas_call(functools.partial(gradient_kernel, n, groups, examples, wi...  56.1 us
    unnamed x5, local copies, waits for them, and re-layouts  9.86 us
    pallas_call x1, Pallas kernels, shards(): pl.pallas_call(functools.partial(score_kernel, n, groups, examples), out_...  6.96 us
    dot_general x1, matrix products, shards(): terms = jnp.einsum('emv,qmv->eq', both, queries, preferred_element_type=f32)  5.14 us

profile of v2, /device:TPU:0, one launch (start us, length us, event | category | flops | bytes accessed | tf_op | source)
XLA Modules:
  0.0 79.2 jit_solution(13563704883138132441)
XLA Ops:
  0.0 1.7 %copy.21.refs_9_ = bf16[1024,64]{1,0:T(8,128)(2,1)} copy(bf16[1024,64]{0,1:T(8,128)(2,1)} %param.20) | data formatting | bytes 262144 | tf_op args[9]
  1.7 2.3 %copy.18.refs_6_ = bf16[3584,64]{1,0:T(8,128)(2,1)} copy(bf16[3584,64]{0,1:T(8,128)(2,1)} %param.17) | data formatting | bytes 917504 | tf_op args[6]
  4.0 2.3 %copy.19.refs_7_ = bf16[3584,64]{1,0:T(8,128)(2,1)} copy(bf16[3584,64]{0,1:T(8,128)(2,1)} %param.18) | data formatting | bytes 917504 | tf_op args[7]
  6.3 2.3 %copy.20.refs_8_ = bf16[3584,64]{1,0:T(8,128)(2,1)} copy(bf16[3584,64]{0,1:T(8,128)(2,1)} %param.19) | data formatting | bytes 917504 | tf_op args[8]
  8.6 56.1 %shard_map.109 = f32[4,2,3,16,64]{4,3,2,1,0:T(8,128)} custom-call(bf16[1024,1024]{1,0:T(8,128)(2,1)} %refs_0_.1, bf16[1024,3584]{1,0:T(8,128)(2,1)} %refs_1_.1, bf16[1024,3584]{1,0:T(8,128)(2,1)} %refs_2_.1, bf16[1024,3584]{1,0:T(8,128)(2,1)} %refs_3_.1, bf16[1024,1024]{1,0:T(8,128)(2,1)} %refs_4_.1, bf16[1024,128]{1,0:T(8,128)(2,1)} %refs_5_.1, ...), custom_call_target="tpu_custom_call" | custom-call | tf_op jit(solution)/shard_map/pallas_call | solution.py:232
  64.7 1.1 %reshape.5 = f32[8,3,1024]{2,1,0:T(4,128)S(1)} reshape(f32[4,2,3,16,64]{4,3,2,1,0:T(8,128)} %shard_map.109) | data formatting | bytes 196608 | tf_op jit(solution)/shard_map/reshape | solution.py:258
  65.7 0.1 reduce-precision_convert_fusion
  65.8 5.1 %convolution_bitcast_fusion.terms = f32[16,1024]{1,0:T(8,128)} fusion(bf16[1024,3,1024]{2,0,1:T(8,128)(2,1)} %param.21, bf16[8,3,1024]{2,0,1:T(8,128)(2,1)S(1)} %get-tuple-element.6, bf16[8,3,1024]{2,0,1:T(8,128)(2,1)S(1)} %get-tuple-element.5), kind=kOutput, calls=%fused_computation | convolution fusion | flops 100859904 | bytes 6455296 | tf_op jit(solution)/shard_map/emv,qmv->eq/dot_general | solution.py:262
  70.9 7.0 %shard_map.110 = f32[2,1024]{1,0:T(2,128)} custom-call(f32[16,1024]{1,0:T(8,128)} %convolution_bitcast_fusion.terms), custom_call_target="tpu_custom_call" | custom-call | tf_op jit(solution)/shard_map/pallas_call | solution.py:264
  77.9 1.3 %copy.27 = f32[2,1024]{1,0:T(2,128)} copy(f32[2,1024]{1,0:T(2,128)} %shard_map.110) | data formatting | bytes 16384

commit v3 on v2

v3 whole, which is shorter than its diff:
```python
import functools

import jax
import jax.numpy as jnp
from jax import lax
from jax.experimental import pallas as pl
from jax.experimental.pallas import tpu as pltpu
from jax.sharding import PartitionSpec as P

LEN = 512
MESH = pl.DeviceIdType.MESH
AHEAD = 2
CHUNKS = 4
CHUNK = LEN // CHUNKS


def gradient_kernel(n, groups, width, *refs):
    values, factors, out = refs[:5], refs[5:10], refs[10]
    held, weights = refs[11:16], refs[16:21]
    (terms, arrived, pieces, shared, load_sem, weight_sem,
     send_sem, recv_sem, spread_send, spread_recv) = refs[21:]
    me, lane = lax.axis_index("tensor"), lax.axis_index("dp")
    rows = width // n
    last = n - 1
    at_end = (me == 0) | (me == last)
    mine = jnp.where(me == 0, 0, 1)

    def load(step, k, example):
        start = pl.multiple_of(example * LEN + step * CHUNK, CHUNK)
        return pltpu.make_async_copy(
            values[k].at[pl.ds(start, CHUNK)],
            held[k].at[step, pl.ds(example * CHUNK, CHUNK)],
            load_sem.at[step, k, example],
        )

    def weight(k):
        return pltpu.make_async_copy(factors[k], weights[k], weight_sem.at[k])

    for step in range(AHEAD):
        for k in range(5):
            if step == 0:
                weight(k).start()
            load(step, k, 0).start()
            load(step, k, 1).start()

    barrier = pltpu.get_barrier_semaphore()

    def greet(there, target):
        @pl.when(there)
        def _():
            pl.semaphore_signal(barrier, inc=1, device_id=target, device_id_type=MESH)

    greet(me > 0, {"dp": lane, "tensor": jnp.maximum(me - 1, 0)})
    greet(me < last, {"dp": lane, "tensor": jnp.minimum(me + 1, last)})
    for b in range(groups):
        for end in (0, last):
            greet(jnp.logical_not((lane == b) & (me == end)), {"dp": b, "tensor": end})

    @pl.when(at_end)
    def _():
        pl.semaphore_wait(barrier, n * groups)

    @pl.when(jnp.logical_not(at_end))
    def _():
        pl.semaphore_wait(barrier, 2)

    for k in range(5):
        weight(k).wait()

    def send(example, chunk):
        target = jnp.maximum(me - 1, 0) if example == 0 else jnp.minimum(me + 1, last)
        return pltpu.make_async_remote_copy(
            src_ref=terms.at[chunk, pl.ds(example * CHUNK, CHUNK)],
            dst_ref=arrived.at[chunk, pl.ds(example * CHUNK, CHUNK)],
            send_sem=send_sem.at[example, chunk],
            recv_sem=recv_sem.at[example, chunk],
            device_id={"dp": lane, "tensor": target},
            device_id_type=MESH,
        )

    def advance(step, carry):
        @pl.when(step + AHEAD < CHUNKS)
        def _():
            for k in range(5):
                load(step + AHEAD, k, 0).start()
                load(step + AHEAD, k, 1).start()

        @pl.when(step < CHUNKS)
        def _():
            column = 0
            for k in range(5):
                load(step, k, 0).wait()
                load(step, k, 1).wait()
                turned = 1 if k else 0
                share = weights[k].shape[1 - turned]
                terms[step, :, column : column + share] = lax.dot_general(
                    held[k][step],
                    weights[k][...],
                    (((1,), (turned,)), ((), ())),
                    preferred_element_type=jnp.float32,
                )
                column += share

        for example in range(2):
            hops = last - me if example == 0 else me
            chunk = step - hops
            part = slice(example * CHUNK, (example + 1) * CHUNK)

            @pl.when((chunk >= 0) & (chunk < CHUNKS))
            def _(example=example, hops=hops, chunk=chunk, part=part):
                @pl.when(hops > 0)
                def _():
                    send(example, chunk).wait_recv()
                    terms[chunk, part, :] = terms[chunk, part, :] + arrived[chunk, part, :]

                @pl.when(hops < last)
                def _():
                    send(example, chunk).start()

        return carry

    lax.fori_loop(0, CHUNKS + last, advance, 0)

    def spread(b, peer):
        return pltpu.make_async_remote_copy(
            src_ref=pieces.at[peer],
            dst_ref=shared.at[lane, mine],
            send_sem=spread_send.at[b, peer],
            recv_sem=spread_recv.at[lane, mine],
            device_id={"dp": b, "tensor": peer},
            device_id_type=MESH,
        )

    def to_others(action):
        def visit(q, carry):
            b, peer = q // n, lax.rem(q, n)

            @pl.when(jnp.logical_not((b == lane) & (peer == me)))
            def _():
                action(spread(b, peer))

            return carry

        lax.fori_loop(0, groups * n, visit, 0)

    @pl.when(at_end)
    def _():
        start = pl.multiple_of(mine * CHUNK, CHUNK)
        total = terms[:, pl.ds(start, CHUNK), :].reshape(LEN, 6 * width)
        product = lax.dot_general(
            total[:, 3 * width :],
            total[:, : 3 * width],
            (((0,), (0,)), ((), ())),
            precision=lax.Precision.HIGHEST,
            preferred_element_type=jnp.float32,
        ) * (LEN ** -0.5)
        for peer in range(n):
            for m in range(3):
                first = m * width + peer * rows
                pieces[peer, m] = product[first : first + rows, m * width : (m + 1) * width]
        to_others(lambda copy: copy.start())
        shared[lane, mine] = pieces[me]

    for b in range(groups):
        for example, end in enumerate((0, last)):
            @pl.when(jnp.logical_not((lane == b) & (me == end)))
            def _(b=b, example=example, end=end):
                pltpu.make_async_remote_copy(
                    src_ref=pieces.at[0],
                    dst_ref=shared.at[b, example],
                    send_sem=spread_send.at[0, 0],
                    recv_sem=spread_recv.at[b, example],
                    device_id={"dp": b, "tensor": end},
                    device_id_type=MESH,
                ).wait_recv()

    out[...] = shared[...]

    @pl.when(at_end)
    def _():
        to_others(lambda copy: copy.wait_send())

    for chunk in range(CHUNKS):
        @pl.when(me > 0)
        def _(chunk=chunk):
            send(0, chunk).wait_send()

        @pl.when(me < last)
        def _(chunk=chunk):
            send(1, chunk).wait_send()


def score_kernel(n, groups, examples, terms, out, blocks, arrived, send_sem, recv_sem):
    me, lane = lax.axis_index("tensor"), lax.axis_index("dp")
    split = n // groups
    columns = out.shape[1]
    source = me // split
    own = lane == source

    barrier = pltpu.get_barrier_semaphore()
    for t in range(n):
        @pl.when(jnp.logical_not(own & (me == t)))
        def _(t=t):
            pl.semaphore_signal(barrier, inc=1, device_id={"dp": source, "tensor": t}, device_id_type=MESH)

    for b in range(groups):
        for s in range(split):
            blocks[b * split + s] = (
                terms[b * examples : (b + 1) * examples, s * columns : (s + 1) * columns]
                + terms[
                    (groups + b) * examples : (groups + b + 1) * examples,
                    s * columns : (s + 1) * columns,
                ]
            )

    @pl.when(own)
    def _():
        pl.semaphore_wait(barrier, n - 1)

    @pl.when(jnp.logical_not(own))
    def _():
        pl.semaphore_wait(barrier, n)

    def send(b, s):
        return pltpu.make_async_remote_copy(
            src_ref=blocks.at[b * split + s],
            dst_ref=arrived.at[me],
            send_sem=send_sem.at[b * split + s],
            recv_sem=recv_sem.at[me],
            device_id={"dp": b, "tensor": lane * split + s},
            device_id_type=MESH,
        )

    def to_me(b, s):
        return (lane == b) & (me == lane * split + s)

    for b in range(groups):
        for s in range(split):
            @pl.when(jnp.logical_not(to_me(b, s)))
            def _(b=b, s=s):
                send(b, s).start()

            @pl.when(to_me(b, s))
            def _(b=b, s=s):
                arrived[me] = blocks[b * split + s]

    def wait_from(t):
        pltpu.make_async_remote_copy(
            src_ref=blocks.at[0],
            dst_ref=arrived.at[t],
            send_sem=send_sem.at[0],
            recv_sem=recv_sem.at[t],
            device_id={"dp": source, "tensor": t},
            device_id_type=MESH,
        ).wait_recv()

    for t in range(n):
        @pl.when(jnp.logical_not(own & (me == t)))
        def _(t=t):
            wait_from(t)

    total = arrived[0]
    for t in range(1, n):
        total = total + arrived[t]
    out[...] = total
    for b in range(groups):
        for s in range(split):
            @pl.when(jnp.logical_not(to_me(b, s)))
            def _(b=b, s=s):
                send(b, s).wait_send()


def shards(n, groups, *arrays):
    values, factors, queries = arrays[:5], arrays[5:10], arrays[10]
    width = factors[1].shape[1]
    local = values[0].shape[0]
    examples, rows = local // LEN, width // n
    f32, bf16 = jnp.float32, jnp.bfloat16
    dma = pltpu.SemaphoreType.DMA
    turned = [factors[0]] + [w.T for w in factors[1:]]
    gradients = pl.pallas_call(
        functools.partial(gradient_kernel, n, groups, width),
        out_shape=jax.ShapeDtypeStruct((groups, examples, 3, rows, width), f32),
        in_specs=[pl.BlockSpec(memory_space=pl.ANY)] * 10,
        out_specs=pl.BlockSpec(memory_space=pltpu.VMEM),
        scratch_shapes=[pltpu.VMEM((CHUNKS, 2 * CHUNK, v.shape[1]), bf16) for v in values]
        + [pltpu.VMEM(w.shape, bf16) for w in turned]
        + [
            pltpu.VMEM((CHUNKS, 2 * CHUNK, 6 * width), f32),
            pltpu.VMEM((CHUNKS, 2 * CHUNK, 6 * width), f32),
            pltpu.VMEM((n, 3, rows, width), f32),
            pltpu.VMEM((groups, examples, 3, rows, width), f32),
            dma((CHUNKS, 5, 2)),
            dma((5,)),
            dma((2, CHUNKS)),
            dma((2, CHUNKS)),
            dma((groups, n)),
            dma((groups, examples)),
        ],
        compiler_params=pltpu.CompilerParams(
            collective_id=0, has_side_effects=True, vmem_limit_bytes=56 * 2**20
        ),
    )(*values, *turned)
    gradients = gradients.reshape(groups * examples, 3, rows * width)
    high = lax.reduce_precision(gradients, 8, 7)
    low = gradients - high
    both = jnp.concatenate([high, low], 0).astype(bf16)
    terms = jnp.einsum("emv,qmv->eq", both, queries, preferred_element_type=f32)
    columns = terms.shape[1] * groups // n
    return pl.pallas_call(
        functools.partial(score_kernel, n, groups, examples),
        out_shape=jax.ShapeDtypeStruct((examples, columns), f32),
        in_specs=[pl.BlockSpec(memory_space=pltpu.VMEM)],
        out_specs=pl.BlockSpec(memory_space=pltpu.VMEM),
        scratch_shapes=[
            pltpu.VMEM((n, examples, columns), f32),
            pltpu.VMEM((n, examples, columns), f32),
            dma((n,)),
            dma((n,)),
        ],
        compiler_params=pltpu.CompilerParams(collective_id=1, has_side_effects=True),
    )(terms)


def solution(mesh):
    placed = (
        P(("parts", "dp"), "tensor"),
        P(("parts", "dp"), "tensor"),
        P(("parts", "dp"), "tensor"),
        P(("parts", "dp"), "tensor"),
        P(("parts", "dp"), "tensor"),
        P("tensor", None),
        P("tensor", None),
        P("tensor", None),
        P("tensor", None),
        P("tensor", None),
        P("dp", None, "tensor"),
    )
    return jax.shard_map(
        functools.partial(shards, mesh.shape["tensor"], mesh.shape["dp"]),
        mesh=mesh,
        in_specs=placed,
        out_specs=P(("parts", "dp"), "tensor"),
        check_vma=False,
    )
```

time: 79.6 us -> 66.1 us (0.83)
  local copies, waits for them, and re-layouts: 10.9 us -> 2.35 us
  Pallas kernels: 63.1 us -> 58.2 us
    unnamed x5 -> x1, local copies, waits for them, and re-layouts: 9.86 us -> 1.3 us
    pallas_call x1, Pallas kernels: 56.1 us -> 49.5 us  [shards(): pl.pallas_call(functools.partial(gradient_kernel, n, groups, width), out_...]
    pallas_call x1, Pallas kernels: 6.96 us -> 8.76 us  [shards(): pl.pallas_call(functools.partial(score_kernel, n, groups, examples), out_...]
where the time goes in v3:
time: 66.1 us; the launch traced here: 65.8 us
  Pallas kernels  58.2 us (88%)
  matrix products  5.14 us (8%)
  local copies, waits for them, and re-layouts  2.35 us (4%)
    pallas_call x1, Pallas kernels, shards(): pl.pallas_call(functools.partial(gradient_kernel, n, groups, width), out_...  49.5 us
    pallas_call x1, Pallas kernels, shards(): pl.pallas_call(functools.partial(score_kernel, n, groups, examples), out_...  8.76 us
    dot_general x1, matrix products, shards(): terms = jnp.einsum('emv,qmv->eq', both, queries, preferred_element_type=f32)  5.14 us

profile of v3, /device:TPU:0, one launch (start us, length us, event | category | flops | bytes accessed | tf_op | source)
XLA Modules:
  0.0 65.8 jit_solution(2211558766002268351)
XLA Ops:
  0.0 49.5 %shard_map.109 = f32[4,2,3,16,64]{4,3,2,1,0:T(8,128)} custom-call(bf16[1024,1024]{1,0:T(8,128)(2,1)} %refs_0_.1, bf16[1024,3584]{1,0:T(8,128)(2,1)} %refs_1_.1, bf16[1024,3584]{1,0:T(8,128)(2,1)} %refs_2_.1, bf16[1024,3584]{1,0:T(8,128)(2,1)} %refs_3_.1, bf16[1024,1024]{1,0:T(8,128)(2,1)} %refs_4_.1, bf16[1024,128]{1,0:T(8,128)(2,1)} %refs_5_.1, ...), custom_call_target="tpu_custom_call" | custom-call | tf_op jit(solution)/shard_map/pallas_call | solution.py:281
  49.5 1.1 %reshape.5 = f32[8,3,1024]{2,1,0:T(4,128)S(1)} reshape(f32[4,2,3,16,64]{4,3,2,1,0:T(8,128)} %shard_map.109) | data formatting | bytes 196608 | tf_op jit(solution)/shard_map/reshape | solution.py:304
  50.5 0.1 reduce-precision_convert_fusion
  50.6 5.1 %convolution_bitcast_fusion.terms = f32[16,1024]{1,0:T(8,128)} fusion(bf16[1024,3,1024]{2,0,1:T(8,128)(2,1)} %param.21, bf16[8,3,1024]{2,0,1:T(8,128)(2,1)S(1)} %get-tuple-element.6, bf16[8,3,1024]{2,0,1:T(8,128)(2,1)S(1)} %get-tuple-element.5), kind=kOutput, calls=%fused_computation | convolution fusion | flops 100859904 | bytes 6455296 | tf_op jit(solution)/shard_map/emv,qmv->eq/dot_general | solution.py:308
  55.8 8.8 %shard_map.110 = f32[2,1024]{1,0:T(2,128)} custom-call(f32[16,1024]{1,0:T(8,128)} %convolution_bitcast_fusion.terms), custom_call_target="tpu_custom_call" | custom-call | tf_op jit(solution)/shard_map/pallas_call | solution.py:310
  64.5 1.3 %copy.19 = f32[2,1024]{1,0:T(2,128)} copy(f32[2,1024]{1,0:T(2,128)} %shard_map.110) | data formatting | bytes 16384

commit v4 on v3

--- a/solution.py
+++ b/solution.py
@@ -12,6 +12,8 @@
 AHEAD = 2
 CHUNKS = 4
 CHUNK = LEN // CHUNKS
+PIECES = 4
+PIECE = CHUNK // PIECES
 
 
 def gradient_kernel(n, groups, width, *refs):
@@ -67,13 +69,14 @@
     for k in range(5):
         weight(k).wait()
 
-    def send(example, chunk):
+    def send(example, chunk, piece):
         target = jnp.maximum(me - 1, 0) if example == 0 else jnp.minimum(me + 1, last)
+        part = pl.ds(example * CHUNK + piece * PIECE, PIECE)
         return pltpu.make_async_remote_copy(
-            src_ref=terms.at[chunk, pl.ds(example * CHUNK, CHUNK)],
-            dst_ref=arrived.at[chunk, pl.ds(example * CHUNK, CHUNK)],
-            send_sem=send_sem.at[example, chunk],
-            recv_sem=recv_sem.at[example, chunk],
+            src_ref=terms.at[chunk, part],
+            dst_ref=arrived.at[chunk, part],
+            send_sem=send_sem.at[example, chunk, piece],
+            recv_sem=recv_sem.at[example, chunk, piece],
             device_id={"dp": lane, "tensor": target},
             device_id_type=MESH,
         )
@@ -101,21 +104,22 @@
                 )
                 column += share
 
-        for example in range(2):
-            hops = last - me if example == 0 else me
-            chunk = step - hops
-            part = slice(example * CHUNK, (example + 1) * CHUNK)
-
-            @pl.when((chunk >= 0) & (chunk < CHUNKS))
-            def _(example=example, hops=hops, chunk=chunk, part=part):
-                @pl.when(hops > 0)
-                def _():
-                    send(example, chunk).wait_recv()
+        for piece in range(PIECES):
+            for example in range(2):
+                hops = last - me if example == 0 else me
+                chunk = step - hops
+                first = example * CHUNK + piece * PIECE
+                part = slice(first, first + PIECE)
+                active = (chunk >= 0) & (chunk < CHUNKS)
+
+                @pl.when(active & (hops > 0))
+                def _(example=example, chunk=chunk, piece=piece, part=part):
+                    send(example, chunk, piece).wait_recv()
                     terms[chunk, part, :] = terms[chunk, part, :] + arrived[chunk, part, :]
 
-                @pl.when(hops < last)
-                def _():
-                    send(example, chunk).start()
+                @pl.when(active & (hops < last))
+                def _(example=example, chunk=chunk, piece=piece):
+                    send(example, chunk, piece).start()
 
         return carry
 
@@ -181,13 +185,14 @@
         to_others(lambda copy: copy.wait_send())
 
     for chunk in range(CHUNKS):
-        @pl.when(me > 0)
-        def _(chunk=chunk):
-            send(0, chunk).wait_send()
-
-        @pl.when(me < last)
-        def _(chunk=chunk):
-            send(1, chunk).wait_send()
+        for piece in range(PIECES):
+            @pl.when(me > 0)
+            def _(chunk=chunk, piece=piece):
+                send(0, chunk, piece).wait_send()
+
+            @pl.when(me < last)
+            def _(chunk=chunk, piece=piece):
+                send(1, chunk, piece).wait_send()
 
 
 def score_kernel(n, groups, examples, terms, out, blocks, arrived, send_sem, recv_sem):
@@ -292,8 +297,8 @@
             pltpu.VMEM((groups, examples, 3, rows, width), f32),
             dma((CHUNKS, 5, 2)),
             dma((5,)),
-            dma((2, CHUNKS)),
-            dma((2, CHUNKS)),
+            dma((2, CHUNKS, PIECES)),
+            dma((2, CHUNKS, PIECES)),
             dma((groups, n)),
             dma((groups, examples)),
         ],

time: 66.1 us -> 65.6 us (level)
    pallas_call x1, Pallas kernels: 49.5 us -> 48.3 us  [shards(): pl.pallas_call(functools.partial(gradient_kernel, n, groups, width), out_...]
    pallas_call x1, Pallas kernels: 8.76 us -> 9.49 us  [shards(): pl.pallas_call(functools.partial(score_kernel, n, groups, examples), out_...]
where the time goes in v4:
time: 65.6 us; the launch traced here: 65.3 us
  Pallas kernels  57.8 us (88%)
  matrix products  5.14 us (8%)
  local copies, waits for them, and re-layouts  2.35 us (4%)
    pallas_call x1, Pallas kernels, shards(): pl.pallas_call(functools.partial(gradient_kernel, n, groups, width), out_...  48.3 us
    pallas_call x1, Pallas kernels, shards(): pl.pallas_call(functools.partial(score_kernel, n, groups, examples), out_...  9.49 us
    dot_general x1, matrix products, shards(): terms = jnp.einsum('emv,qmv->eq', both, queries, preferred_element_type=f32)  5.14 us

profile of v4, /device:TPU:0, one launch (start us, length us, event | category | flops | bytes accessed | tf_op | source)
XLA Modules:
  0.0 65.3 jit_solution(1642350814061190856)
XLA Ops:
  0.0 48.3 %shard_map.109 = f32[4,2,3,16,64]{4,3,2,1,0:T(8,128)} custom-call(bf16[1024,1024]{1,0:T(8,128)(2,1)} %refs_0_.1, bf16[1024,3584]{1,0:T(8,128)(2,1)} %refs_1_.1, bf16[1024,3584]{1,0:T(8,128)(2,1)} %refs_2_.1, bf16[1024,3584]{1,0:T(8,128)(2,1)} %refs_3_.1, bf16[1024,1024]{1,0:T(8,128)(2,1)} %refs_4_.1, bf16[1024,128]{1,0:T(8,128)(2,1)} %refs_5_.1, ...), custom_call_target="tpu_custom_call" | custom-call | tf_op jit(solution)/shard_map/pallas_call | solution.py:286
  48.3 1.1 %reshape.5 = f32[8,3,1024]{2,1,0:T(4,128)S(1)} reshape(f32[4,2,3,16,64]{4,3,2,1,0:T(8,128)} %shard_map.109) | data formatting | bytes 196608 | tf_op jit(solution)/shard_map/reshape | solution.py:309
  49.3 0.1 reduce-precision_convert_fusion
  49.4 5.1 %convolution_bitcast_fusion.terms = f32[16,1024]{1,0:T(8,128)} fusion(bf16[1024,3,1024]{2,0,1:T(8,128)(2,1)} %param.21, bf16[8,3,1024]{2,0,1:T(8,128)(2,1)S(1)} %get-tuple-element.6, bf16[8,3,1024]{2,0,1:T(8,128)(2,1)S(1)} %get-tuple-element.5), kind=kOutput, calls=%fused_computation | convolution fusion | flops 100859904 | bytes 6455296 | tf_op jit(solution)/shard_map/emv,qmv->eq/dot_general | solution.py:313
  54.5 9.5 %shard_map.110 = f32[2,1024]{1,0:T(2,128)} custom-call(f32[16,1024]{1,0:T(8,128)} %convolution_bitcast_fusion.terms), custom_call_target="tpu_custom_call" | custom-call | tf_op jit(solution)/shard_map/pallas_call | solution.py:315
  64.0 1.3 %copy.19 = f32[2,1024]{1,0:T(2,128)} copy(f32[2,1024]{1,0:T(2,128)} %shard_map.110) | data formatting | bytes 16384

commit v5 on v4

--- a/solution.py
+++ b/solution.py
@@ -9,7 +9,7 @@
 
 LEN = 512
 MESH = pl.DeviceIdType.MESH
-AHEAD = 2
+AHEAD = 1
 CHUNKS = 4
 CHUNK = LEN // CHUNKS
 PIECES = 4
@@ -20,7 +20,8 @@
     values, factors, out = refs[:5], refs[5:10], refs[10]
     held, weights = refs[11:16], refs[16:21]
     (terms, arrived, pieces, shared, load_sem, weight_sem,
-     send_sem, recv_sem, spread_send, spread_recv) = refs[21:]
+     send_sem, recv_sem, spread_send, spread_recv) = refs[21:31]
+    upright = refs[31:]
     me, lane = lax.axis_index("tensor"), lax.axis_index("dp")
     rows = width // n
     last = n - 1
@@ -68,6 +69,8 @@
 
     for k in range(5):
         weight(k).wait()
+        if k:
+            upright[k - 1][...] = weights[k][...].T
 
     def send(example, chunk, piece):
         target = jnp.maximum(me - 1, 0) if example == 0 else jnp.minimum(me + 1, last)
@@ -82,24 +85,24 @@
         )
 
     def advance(step, carry):
-        @pl.when(step + AHEAD < CHUNKS)
-        def _():
-            for k in range(5):
-                load(step + AHEAD, k, 0).start()
-                load(step + AHEAD, k, 1).start()
-
         @pl.when(step < CHUNKS)
         def _():
             column = 0
             for k in range(5):
                 load(step, k, 0).wait()
                 load(step, k, 1).wait()
+
+                @pl.when(step + AHEAD < CHUNKS)
+                def _(k=k):
+                    load(step + AHEAD, k, 0).start()
+                    load(step + AHEAD, k, 1).start()
+
                 turned = 1 if k else 0
                 share = weights[k].shape[1 - turned]
                 terms[step, :, column : column + share] = lax.dot_general(
                     held[k][step],
-                    weights[k][...],
-                    (((1,), (turned,)), ((), ())),
+                    upright[k - 1][...] if k else weights[k][...],
+                    (((1,), (0,)), ((), ())),
                     preferred_element_type=jnp.float32,
                 )
                 column += share
@@ -301,7 +304,8 @@
             dma((2, CHUNKS, PIECES)),
             dma((groups, n)),
             dma((groups, examples)),
-        ],
+        ]
+        + [pltpu.VMEM(w.shape, bf16) for w in factors[1:]],
         compiler_params=pltpu.CompilerParams(
             collective_id=0, has_side_effects=True, vmem_limit_bytes=56 * 2**20
         ),

time: 65.6 us -> 61.2 us (0.933)
  Pallas kernels: 57.8 us -> 53.4 us
    pallas_call x1, Pallas kernels: 48.3 us -> 44.9 us  [shards(): pl.pallas_call(functools.partial(gradient_kernel, n, groups, width), out_...]
    pallas_call x1, Pallas kernels: 9.49 us -> 8.44 us  [shards(): pl.pallas_call(functools.partial(score_kernel, n, groups, examples), out_...]
where the time goes in v5:
time: 61.2 us; the launch traced here: 60.9 us
  Pallas kernels  53.4 us (87%)
  matrix products  5.14 us (8%)
  local copies, waits for them, and re-layouts  2.35 us (4%)
    pallas_call x1, Pallas kernels, shards(): pl.pallas_call(functools.partial(gradient_kernel, n, groups, width), out_...  44.9 us
    pallas_call x1, Pallas kernels, shards(): pl.pallas_call(functools.partial(score_kernel, n, groups, examples), out_...  8.44 us
    dot_general x1, matrix products, shards(): terms = jnp.einsum('emv,qmv->eq', both, queries, preferred_element_type=f32)  5.14 us
    unnamed x1, local copies, waits for them, and re-layouts  1.3 us

profile of v5, /device:TPU:0, one launch (start us, length us, event | category | flops | bytes accessed | tf_op | source)
XLA Modules:
  0.0 60.9 jit_solution(4549967610998986527)
XLA Ops:
  0.0 44.9 %shard_map.109 = f32[4,2,3,16,64]{4,3,2,1,0:T(8,128)} custom-call(bf16[1024,1024]{1,0:T(8,128)(2,1)} %refs_0_.1, bf16[1024,3584]{1,0:T(8,128)(2,1)} %refs_1_.1, bf16[1024,3584]{1,0:T(8,128)(2,1)} %refs_2_.1, bf16[1024,3584]{1,0:T(8,128)(2,1)} %refs_3_.1, bf16[1024,1024]{1,0:T(8,128)(2,1)} %refs_4_.1, bf16[1024,128]{1,0:T(8,128)(2,1)} %refs_5_.1, ...), custom_call_target="tpu_custom_call" | custom-call | tf_op jit(solution)/shard_map/pallas_call | solution.py:289
  44.9 1.1 %reshape.5 = f32[8,3,1024]{2,1,0:T(4,128)S(1)} reshape(f32[4,2,3,16,64]{4,3,2,1,0:T(8,128)} %shard_map.109) | data formatting | bytes 196608 | tf_op jit(solution)/shard_map/reshape | solution.py:313
  46.0 0.1 reduce-precision_convert_fusion
  46.1 5.1 %convolution_bitcast_fusion.terms = f32[16,1024]{1,0:T(8,128)} fusion(bf16[1024,3,1024]{2,0,1:T(8,128)(2,1)} %param.21, bf16[8,3,1024]{2,0,1:T(8,128)(2,1)S(1)} %get-tuple-element.6, bf16[8,3,1024]{2,0,1:T(8,128)(2,1)S(1)} %get-tuple-element.5), kind=kOutput, calls=%fused_computation | convolution fusion | flops 100859904 | bytes 6455296 | tf_op jit(solution)/shard_map/emv,qmv->eq/dot_general | solution.py:317
  51.2 8.4 %shard_map.110 = f32[2,1024]{1,0:T(2,128)} custom-call(f32[16,1024]{1,0:T(8,128)} %convolution_bitcast_fusion.terms), custom_call_target="tpu_custom_call" | custom-call | tf_op jit(solution)/shard_map/pallas_call | solution.py:319
  59.6 1.3 %copy.19 = f32[2,1024]{1,0:T(2,128)} copy(f32[2,1024]{1,0:T(2,128)} %shard_map.110) | data formatting | bytes 16384

commit v6 on v5

--- a/solution.py
+++ b/solution.py
@@ -59,18 +59,18 @@
         for end in (0, last):
             greet(jnp.logical_not((lane == b) & (me == end)), {"dp": b, "tensor": end})
 
-    @pl.when(at_end)
-    def _():
-        pl.semaphore_wait(barrier, n * groups)
-
-    @pl.when(jnp.logical_not(at_end))
-    def _():
-        pl.semaphore_wait(barrier, 2)
-
     for k in range(5):
         weight(k).wait()
         if k:
             upright[k - 1][...] = weights[k][...].T
+
+    @pl.when(at_end)
+    def _():
+        pl.semaphore_wait(barrier, n * groups)
+
+    @pl.when(jnp.logical_not(at_end))
+    def _():
+        pl.semaphore_wait(barrier, 2)
 
     def send(example, chunk, piece):
         target = jnp.maximum(me - 1, 0) if example == 0 else jnp.minimum(me + 1, last)

time: 61.2 us -> 61.2 us (level)
    pallas_call x1, Pallas kernels: 44.9 us -> 44 us  [shards(): pl.pallas_call(functools.partial(gradient_kernel, n, groups, width), out_...]
    pallas_call x1, Pallas kernels: 8.44 us -> 9.35 us  [shards(): pl.pallas_call(functools.partial(score_kernel, n, groups, examples), out_...]
where the time goes in v6:
time: 61.2 us; the launch traced here: 60.9 us
  Pallas kernels  53.4 us (87%)
  matrix products  5.14 us (8%)
  local copies, waits for them, and re-layouts  2.35 us (4%)
    pallas_call x1, Pallas kernels, shards(): pl.pallas_call(functools.partial(gradient_kernel, n, groups, width), out_...  44 us
    pallas_call x1, Pallas kernels, shards(): pl.pallas_call(functools.partial(score_kernel, n, groups, examples), out_...  9.35 us
    dot_general x1, matrix products, shards(): terms = jnp.einsum('emv,qmv->eq', both, queries, preferred_element_type=f32)  5.14 us
    unnamed x1, local copies, waits for them, and re-layouts  1.3 us

profile of v6, /device:TPU:0, one launch (start us, length us, event | category | flops | bytes accessed | tf_op | source)
XLA Modules:
  0.0 60.9 jit_solution(9715270284774554868)
XLA Ops:
  0.0 44.0 %shard_map.109 = f32[4,2,3,16,64]{4,3,2,1,0:T(8,128)} custom-call(bf16[1024,1024]{1,0:T(8,128)(2,1)} %refs_0_.1, bf16[1024,3584]{1,0:T(8,128)(2,1)} %refs_1_.1, bf16[1024,3584]{1,0:T(8,128)(2,1)} %refs_2_.1, bf16[1024,3584]{1,0:T(8,128)(2,1)} %refs_3_.1, bf16[1024,1024]{1,0:T(8,128)(2,1)} %refs_4_.1, bf16[1024,128]{1,0:T(8,128)(2,1)} %refs_5_.1, ...), custom_call_target="tpu_custom_call" | custom-call | tf_op jit(solution)/shard_map/pallas_call | solution.py:289
  44.0 1.1 %reshape.5 = f32[8,3,1024]{2,1,0:T(4,128)S(1)} reshape(f32[4,2,3,16,64]{4,3,2,1,0:T(8,128)} %shard_map.109) | data formatting | bytes 196608 | tf_op jit(solution)/shard_map/reshape | solution.py:313
  45.1 0.1 reduce-precision_convert_fusion
  45.1 5.1 %convolution_bitcast_fusion.terms = f32[16,1024]{1,0:T(8,128)} fusion(bf16[1024,3,1024]{2,0,1:T(8,128)(2,1)} %param.21, bf16[8,3,1024]{2,0,1:T(8,128)(2,1)S(1)} %get-tuple-element.6, bf16[8,3,1024]{2,0,1:T(8,128)(2,1)S(1)} %get-tuple-element.5), kind=kOutput, calls=%fused_computation | convolution fusion | flops 100859904 | bytes 6455296 | tf_op jit(solution)/shard_map/emv,qmv->eq/dot_general | solution.py:317
  50.3 9.3 %shard_map.110 = f32[2,1024]{1,0:T(2,128)} custom-call(f32[16,1024]{1,0:T(8,128)} %convolution_bitcast_fusion.terms), custom_call_target="tpu_custom_call" | custom-call | tf_op jit(solution)/shard_map/pallas_call | solution.py:319
  59.6 1.3 %copy.19 = f32[2,1024]{1,0:T(2,128)} copy(f32[2,1024]{1,0:T(2,128)} %shard_map.110) | data formatting | bytes 16384
